TPU v7x, 256 devices: a whole 4x4x8 slice. The times are simulated.
256 devices in a mesh: chan: 32 (over z, y_lo, core), rec: 8 (over y_hi, x).
Axes of the slice: x: 4, y: 4 (y_hi: 2, y_lo: 2; y = y_hi * 2 + y_lo), z: 8, core: 2. Of those that a mesh axis runs over, the one named last changes fastest.
Arguments:
- record: bfloat16 [8192, 64, 2000], P('chan', 'rec'), may hold values from -6 to 6
Outputs:
- stacked: float32 [64, 2, 2, 8192, 128], P('rec', None, None, 'chan')
All inputs are finite; a program needn't handle non-finite values.
Results may differ from a plain program's by a relative error of at most 0.0047.
Values may be sent and summed in bfloat16 or wider, within the bound.
No kernel may reach another device: no remote copies, remote signals or barrier semaphores. Data moves between devices by JAX's collectives and lax.ppermute only.
A program may use at most 128 MiB of HBM per device.

v0:
```python
import math

import jax
import jax.numpy as jnp
from jax import lax
from jax.sharding import PartitionSpec as P

SAMPLES = 2000
WIDE = 512
BINS = 64
FIRST_BIN = 40
BLOCK = 128


def shifted(value, axis, steps):
    count = lax.axis_size(axis)
    initial, last = (max(0, -steps), min(count, count - steps))
    return lax.ppermute(value, axis, [(source, source + steps) for source in range(initial, last)])


def make_table():
    sample = jnp.arange(SAMPLES, dtype=jnp.int32)
    freq = jnp.arange(1, WIDE + 1, dtype=jnp.int32)
    phase = sample[:, None] * freq[None, :] % SAMPLES
    angle = 2.0 * math.pi / SAMPLES * phase.astype(jnp.float32)
    return jnp.concatenate([jnp.cos(angle), -jnp.sin(angle)], axis=1).astype(jnp.bfloat16)


def whiten(spectrum):
    real_part = spectrum[:, :WIDE]
    imag_part = spectrum[:, WIDE:]
    power = real_part * real_part + imag_part * imag_part
    padded = jnp.pad(power, ((0, 0), (1, 1)))
    smooth = (padded[:, :-2] + padded[:, 1:-1] + padded[:, 2:]) / 3.0
    level = jnp.mean(power, axis=1, keepdims=True)
    scale = lax.rsqrt(0.5 * smooth + level + 1e-06)
    low = FIRST_BIN
    high = FIRST_BIN + BINS
    kept_scale = scale[:, low:high]
    return jnp.concatenate(
        [real_part[:, low:high] * kept_scale, imag_part[:, low:high] * kept_scale], axis=1
    ).astype(jnp.bfloat16)


def cross_stack(own, edge, records):
    freqs, _, recs, chans = own.shape
    width = edge.shape[3]
    before = jnp.concatenate([edge, own[..., : chans - width]], axis=3)
    mine = own.reshape(freqs, 2, recs, chans // width, width)
    prior = before.reshape(freqs, 2, recs, chans // width, width)
    left = jnp.concatenate([mine[:, 0], mine[:, 1]], axis=1)
    kinds = []
    for partner in (mine, prior):
        right_real = jnp.concatenate([partner[:, 0], partner[:, 1]], axis=1)
        right_imag = jnp.concatenate([-partner[:, 1], partner[:, 0]], axis=1)
        real_sum = jnp.einsum(
            "frbi,frbj->fbij", left, right_real, preferred_element_type=jnp.float32
        )
        imag_sum = jnp.einsum(
            "frbi,frbj->fbij", left, right_imag, preferred_element_type=jnp.float32
        )
        kinds.append(jnp.stack([real_sum, imag_sum], axis=1))
    result = jnp.stack(kinds, axis=1)
    return result.reshape(freqs, 2, 2, chans, width) / records


def shards(record):
    chans, recs, samples = record.shape
    table = make_table()
    spectrum = jnp.dot(
        record.reshape(chans * recs, samples), table, preferred_element_type=jnp.float32
    )
    white = whiten(spectrum)
    spectra = white.reshape(chans, recs, 2, BINS).transpose(3, 2, 1, 0)
    edge = shifted(spectra[..., chans - BLOCK :], "chan", 1)
    groups = lax.axis_size("rec")
    records = float(recs * groups)
    return lax.psum_scatter(
        cross_stack(spectra, edge, records), "rec", scatter_dimension=0, tiled=True
    )


def solution(mesh):
    in_specs = (P("chan", "rec", None),)
    out_specs = P("rec", None, None, "chan", None)
    return jax.shard_map(shards, mesh=mesh, in_specs=in_specs, out_specs=out_specs, check_vma=False)
```

profile of v0, /device:TPU:128, one launch (start us, length us, event | category | flops | bytes accessed | tf_op | source)
XLA Modules:
  0.0 456.5 jit_solution(11914449245916532215)
XLA Ops:
  6.5 0.0 reduce-scatter.2.cloned.1.call-start
  6.5 18.2 %cosine_convert_fusion = (bf16[2000,512]{1,0:T(8,128)(2,1)S(1)}, bf16[2000,512]{1,0:T(8,128)(2,1)}) fusion(s32[512]{0:T(512)S(1)} %iota_add_fusion), kind=kLoop, calls=%fused_computation.14 | loop fusion | flops 12288000 | bytes 4098048 | tf_op jit(solution)/shard_map/convert.2
  24.8 12.5 %copy.6 = bf16[256,8,2000]{2,1,0:T(8,128)(2,1)} copy(bf16[256,8,2000]{0,2,1:T(8,128)(2,1)} %param.1) | data formatting | bytes 16384000 | tf_op args[0]
  37.3 12.0 %fusion.2 = f32[2048,1024]{0,1:T(8,128)S(1)} fusion(bf16[256,8,2000]{2,1,0:T(8,128)(2,1)} %copy.6, bf16[2000,512]{1,0:T(8,128)(2,1)} %get-tuple-element.18, bf16[2000,512]{1,0:T(8,128)(2,1)S(1)} %get-tuple-element.17), kind=kOutput, calls=%fused_computation.4 | convolution fusion | flops 8396800000 | bytes 20676608 | tf_op jit(solution)/shard_map/dot_general | solution.py:70
  49.3 1.4 fusion.40
  50.7 1.4 pad_slice_fusion.1
  52.1 0.2 fusion.19
  52.3 0.1 fusion.14
  52.4 0.3 copy.7
  52.7 0.4 convert_element_type.14
  53.1 0.7 fusion.42
  53.8 2.1 collective-permute-start
  55.9 1.3 copy.8
  57.3 9.2 %collective-permute-done = bf16[64,2,8,128]{0,1,2,3:T(2,128)(2,1)S(1)} collective-permute-done((bf16[64,2,8,128]{0,1,2,3:T(2,128)(2,1)S(1)}, bf16[64,2,8,128]{0,1,2,3:T(2,128)(2,1)S(1)}, u32[]{:S(2)}, u32[]{:S(2)}) %collective-permute-start) | collective-permute-done | bytes 262176 | tf_op jit(solution)/shard_map/ppermute | solution.py:18
  66.4 1.6 pad_maximum_fusion
  68.0 1.3 copy.13
  69.4 0.2 slice_bitcast_fusion
  69.6 1.3 fusion.36
  70.9 1.3 fusion.24
  72.2 1.3 fusion.28
  73.5 1.3 fusion.20
  74.8 11.1 %maximum_multiply_fusion = f32[64,2,2,256,128]{4,3,2,1,0:T(8,128)} fusion(f32[64,1,1,256,128]{4,3,2,1,0:T(8,128)S(1)} %bitcast.44, f32[64,1,1,256,128]{4,3,2,1,0:T(8,128)S(1)} %bitcast.43, f32[64,1,1,256,128]{4,3,2,1,0:T(8,128)S(1)} %bitcast.45, f32[64,1,1,256,128]{4,3,2,1,0:T(8,128)S(1)} %bitcast.42), kind=kLoop, calls=%fused_computation | loop fusion | flops 33554432 | bytes 67108864 | tf_op jit(solution)/shard_map/div | solution.py:64
  85.8 0.0 reduce-scatter.2.cloned.1.call-update
  85.9 363.8 %reduce-scatter.2.cloned.1.call-done = f32[8,2,2,256,128]{4,3,2,1,0:T(8,128)} async-done(((f32[64,2,2,256,128]{4,3,2,1,0:T(8,128)}), f32[8,2,2,256,128]{4,3,2,1,0:T(8,128)}) %reduce-scatter.2.cloned.1.call-update) | async-done | bytes 4194320 | tf_op jit(solution)/shard_map/reduce_scatter | solution.py:78
  (5 shorter events, 0.1 us)
Async XLA Ops:
  6.5 443.1 %reduce-scatter.2.cloned.1.call-start = ((), (), s32[]{:S(2)}) async-start(), calls=%async_computation.1 | async-start | bytes 37748736 | tf_op jit(solution)/shard_map/reduce_scatter | solution.py:78
  53.8 12.6 %collective-permute-start = (bf16[64,2,8,128]{0,1,2,3:T(2,128)(2,1)S(1)}, bf16[64,2,8,128]{0,1,2,3:T(2,128)(2,1)S(1)}, u32[]{:S(2)}, u32[]{:S(2)}) collective-permute-start(bf16[64,2,8,128]{0,1,2,3:T(2,128)(2,1)S(1)} %get-tuple-element.11), channel_id=1, source_target_pairs={{0,8},{8,16},{16,24},{24,32},{32,40},{40,48},{48,56},{56,64},{64,7... | collective-permute-start | bytes 786440 | tf_op jit(solution)/shard_map/ppermute | solution.py:18
Sparse Core Ops, SparseCore 0:
  86.0 363.6 reduce-scatter.1
where the time goes:
time: 458 us; the launch traced here: 456 us
  waiting for transfers between devices  373 us (81%)
  other arithmetic  32.6 us (7%)
  local copies, waits for them, and re-layouts  18.1 us (4%)
  matrix products  17.2 us (4%)
  between operations  13.5 us (3%)
    reduce_scatter x1, waiting for transfers between devices, shards(): lax.psum_scatter(cross_stack(spectra, edge, records), 'rec', scatter_dime...  364 us
    another operation x3, other arithmetic  18.4 us
    unnamed x1, local copies, waits for them, and re-layouts  12.5 us
    dot_general x1, matrix products, shards(): jnp.dot(record.reshape(chans * recs, samples), table, preferred_element_t...  12 us
    div x1, other arithmetic, cross_stack(): return result.reshape(freqs, 2, 2, chans, width) / records  11.1 us
  transfers between devices with their start and end apart: 2, of which 2 were waited for; matrix products, arithmetic and copies ran while one was open for 0% of the time, Pallas kernels for 0%

commit v1 on v0

v1 whole, which is shorter than its diff:
```python
import functools

import jax
import jax.numpy as jnp
import numpy as np
from jax import lax
from jax.experimental import pallas as pl
from jax.experimental.pallas import tpu as pltpu
from jax.sharding import PartitionSpec as P

SAMPLES = 2000
WIDE = 512
BINS = 64
FIRST_BIN = 40
BLOCK = 128
LOW = FIRST_BIN - 8
HIGH = FIRST_BIN + BINS + 8
NEAR = HIGH - LOW


def make_table():
    sample = np.arange(SAMPLES, dtype=np.int32)
    freq = np.arange(1, WIDE + 1, dtype=np.int32)
    phase = freq[:, None] * sample[None, :] % SAMPLES
    angle = np.float32(2.0 * np.pi / SAMPLES) * phase.astype(np.float32)
    real_part, imag_part = np.cos(angle), -np.sin(angle)
    far = np.r_[0:LOW, HIGH:WIDE]
    rows = [real_part[LOW:HIGH], imag_part[LOW:HIGH], real_part[far], imag_part[far]]
    return np.concatenate(rows, axis=0).astype(jnp.bfloat16)


def shifted(value, axis, steps):
    count = lax.axis_size(axis)
    return lax.ppermute(value, axis, [(source, source + steps) for source in range(count - steps)])


def spectra_kernel(table_ref, record_ref, out_ref, white_ref):
    step = pl.program_id(0)
    rows = record_ref[0]
    near = jnp.dot(table_ref[: 2 * NEAR], rows, preferred_element_type=jnp.float32)
    far = jnp.dot(table_ref[2 * NEAR :], rows, preferred_element_type=jnp.float32)
    real_part, imag_part = near[:NEAR], near[NEAR:]
    power = real_part * real_part + imag_part * imag_part
    total = jnp.sum(power, axis=0, keepdims=True) + jnp.sum(far * far, axis=0, keepdims=True)
    level = total * (1.0 / WIDE)
    smooth = (power[7 : 7 + BINS] + power[8 : 8 + BINS] + power[9 : 9 + BINS]) / 3.0
    scale = lax.rsqrt(0.5 * smooth + level + 1e-06)
    base = pl.multiple_of(step * 2 * BINS, 2 * BINS)
    white = [part[8 : 8 + BINS] * scale for part in (real_part, imag_part)]
    for tile in range(white_ref.shape[0]):
        lanes = slice(tile * 128, (tile + 1) * 128)
        for part in range(2):
            white_ref[tile, pl.ds(base + part * BINS, BINS), :] = white[part][:, lanes]

    @pl.when(step == pl.num_programs(0) - 1)
    def _():
        recs = out_ref.shape[1] // 2
        for index in range(BINS):
            for tile in range(white_ref.shape[0]):
                pair = [
                    white_ref[tile, pl.ds(index + part * BINS, recs, stride=2 * BINS), :]
                    for part in range(2)
                ]
                lanes = slice(tile * 128, (tile + 1) * 128)
                out_ref[index, :, lanes] = jnp.concatenate(pair, axis=0).astype(jnp.bfloat16)


def spectra(table, record):
    recs, samples, chans = record.shape
    return pl.pallas_call(
        spectra_kernel,
        grid=(recs,),
        in_specs=[
            pl.BlockSpec((2 * WIDE, samples), lambda r: (0, 0)),
            pl.BlockSpec((1, samples, chans), lambda r: (r, 0, 0)),
        ],
        out_specs=pl.BlockSpec((BINS, 2 * recs, chans), lambda r: (0, 0, 0)),
        out_shape=jax.ShapeDtypeStruct((BINS, 2 * recs, chans), jnp.bfloat16),
        scratch_shapes=[pltpu.VMEM((chans // 128, recs * 2 * BINS, 128), jnp.float32)],
        compiler_params=pltpu.CompilerParams(vmem_limit_bytes=48 * 2**20),
        cost_estimate=pl.CostEstimate(
            flops=2 * recs * samples * chans * 2 * WIDE,
            bytes_accessed=recs * samples * chans * 2,
            transcendentals=0,
        ),
        name="spectra",
    )(table, record)


def cross_kernel(scale, own_ref, edge_ref, out_ref):
    groups, _, depth, chans = own_ref.shape
    recs = depth // 2
    own = own_ref[:, 0]
    edge = edge_ref[:, 0]

    def turned(value):
        return jnp.concatenate([-value[:, recs:], value[:, :recs]], axis=1)

    def flat(value):
        return value.reshape(groups * depth, value.shape[-1])

    left = flat(own)
    right = [flat(edge), left]
    right_turned = [flat(turned(edge)), flat(turned(own))]
    for block in range(chans // BLOCK):
        here = slice(block * BLOCK, (block + 1) * BLOCK)
        if block == 0:
            prior = right[0], right_turned[0]
        else:
            before = slice((block - 1) * BLOCK, block * BLOCK)
            prior = right[1][:, before], right_turned[1][:, before]
        partners = jnp.concatenate(
            [right[1][:, here], right_turned[1][:, here], prior[0], prior[1]], axis=1
        )
        sums = lax.dot_general(
            left[:, here], partners, (((0,), (0,)), ((), ())), preferred_element_type=jnp.float32
        )
        for kind in range(2):
            for part in range(2):
                first = (2 * kind + part) * BLOCK
                out_ref[0, kind, part, here, :] = sums[:, first : first + BLOCK] * scale


def cross_stack(own, edge, records):
    groups, freqs, depth, chans = own.shape
    return pl.pallas_call(
        functools.partial(cross_kernel, 1.0 / records),
        grid=(freqs,),
        in_specs=[
            pl.BlockSpec((groups, 1, depth, chans), lambda f: (0, f, 0, 0)),
            pl.BlockSpec((groups, 1, depth, BLOCK), lambda f: (0, f, 0, 0)),
        ],
        out_specs=pl.BlockSpec((1, 2, 2, chans, BLOCK), lambda f: (f, 0, 0, 0, 0)),
        out_shape=jax.ShapeDtypeStruct((freqs, 2, 2, chans, BLOCK), jnp.float32),
        name="cross",
    )(own, edge)


def shards(record):
    chans, recs, samples = record.shape
    groups = lax.axis_size("rec")
    white = spectra(jnp.asarray(make_table()), record.transpose(1, 2, 0))
    white = white.reshape(groups, BINS // groups, 2 * recs, chans)
    own = lax.all_to_all(white, "rec", 0, 0, tiled=True)
    edge = shifted(own[..., chans - BLOCK :], "chan", 1)
    return cross_stack(own, edge, float(recs * groups))


def solution(mesh):
    in_specs = (P("chan", "rec", None),)
    out_specs = P("rec", None, None, "chan", None)
    return jax.shard_map(shards, mesh=mesh, in_specs=in_specs, out_specs=out_specs, check_vma=False)
```

time: 458 us -> 50.7 us (0.11)
  waiting for transfers between devices: 373 us -> 7.87 us
  other arithmetic: 32.6 us -> 0 us
  Pallas kernels: 0 us -> 19.2 us
  blocking collectives: 0 us -> 18.3 us
  matrix products: 17.2 us -> 0 us
  local copies, waits for them, and re-layouts: 18.1 us -> 2.93 us
  between operations: 13.5 us -> 0.03 us
    reduce_scatter x1 -> x0, waiting for transfers between devices: 364 us -> none  [shards(): lax.psum_scatter(cross_stack(spectra, edge, records), 'rec', scatter_dime...]
    pallas_call x0 -> x2, Pallas kernels: none -> 19.2 us  [the longest x1 12.9 us: spectra(): pl.pallas_call(spectra_kernel, grid=(recs,), in_specs=[pl.BlockSpec((2 *...]
    another operation x3 -> x0, other arithmetic: 18.4 us -> none
    all_to_all x0 -> x1, blocking collectives: none -> 18.3 us  [shards(): own = lax.all_to_all(white, 'rec', 0, 0, tiled=True)]
    dot_general x5 -> x0, matrix products: 17.2 us -> none  [the longest x1 12 us: shards(): jnp.dot(record.reshape(chans * recs, samples), table, preferred_element_t...]
    div x2 -> x0, other arithmetic: 11.1 us -> none  [the longest x1 11.1 us: cross_stack(): return result.reshape(freqs, 2, 2, chans, width) / records]
    unnamed x1 -> x6, local copies, waits for them, and re-layouts: 12.5 us -> 2.88 us
  transfers between devices with their start and end apart: 2 -> 1, of which waited for: 2 -> 1; matrix products, arithmetic and copies ran while one was open for 0% -> 0% of each run, Pallas kernels for 0% -> 0%
where the time goes in v1:
time: 50.7 us; the launch traced here: 50.2 us
  Pallas kernels  19.2 us (38%)
  blocking collectives  18.3 us (36%)
  waiting for transfers between devices  7.87 us (16%)
  local copies, waits for them, and re-layouts  2.93 us (6%)
  starting transfers between devices  1.92 us (4%)
    all_to_all x1, blocking collectives, shards(): own = lax.all_to_all(white, 'rec', 0, 0, tiled=True)  18.3 us
    pallas_call x1, Pallas kernels, spectra(): pl.pallas_call(spectra_kernel, grid=(recs,), in_specs=[pl.BlockSpec((2 *...  12.9 us
    ppermute x1, waiting for transfers between devices, shifted(): lax.ppermute(value, axis, [(source, source + steps) for source in range(c...  7.87 us
    pallas_call x1, Pallas kernels, cross_stack(): pl.pallas_call(functools.partial(cross_kernel, 1.0 / records), grid=(freq...  6.24 us
    unnamed x6, local copies, waits for them, and re-layouts  2.88 us
    ppermute x1, starting transfers between devices, shifted(): lax.ppermute(value, axis, [(source, source + steps) for source in range(c...  1.92 us
  transfers between devices with their start and end apart: 1, of which 1 were waited for; matrix products, arithmetic and copies ran while one was open for 0% of the time, Pallas kernels for 0%

profile of v1, /device:TPU:128, one launch (start us, length us, event | category | flops | bytes accessed | tf_op | source)
XLA Modules:
  0.0 50.2 jit_solution(8606440104521175931)
XLA Ops:
  0.0 0.0 copy-start
  0.0 2.2 %copy-done = bf16[1024,2000]{1,0:T(8,128)(2,1)S(1)} copy-done((bf16[1024,2000]{1,0:T(8,128)(2,1)S(1)}, bf16[1024,2000]{1,0:T(8,128)(2,1)}, u32[]{:S(2)}) %copy-start) | copy-done | bytes 4096024
  2.2 12.9 %spectra.1 = bf16[64,16,256]{2,1,0:T(8,128)(2,1)S(1)} custom-call(bf16[1024,2000]{1,0:T(8,128)(2,1)S(1)} %copy-done, bf16[8,2000,256]{2,1,0:T(8,128)(2,1)} %bitcast.3), custom_call_target="tpu_custom_call" | custom-call | flops 8388608000 | bytes 8192000 | tf_op jit(solution)/shard_map/spectra/pallas_call | solution.py:70
  15.1 18.3 %all_to_all.5.own_ref = bf16[8,8,16,256]{3,2,1,0:T(8,128)(2,1)S(1)} all-to-all(bf16[8,8,16,256]{3,2,1,0:T(8,128)(2,1)S(1)} %bitcast.2), channel_id=1, replica_groups=mesh['chan'=32,'rec'=8] {'rec'}, dimensions={0} | all-to-all | bytes 1048576 | tf_op jit(solution)/shard_map/all_to_all | solution.py:144
  33.4 0.0 copy-start.1
  33.5 1.9 %collective-permute-start = (bf16[8,8,16,128]{3,2,1,0:T(8,128)(2,1)S(1)}, bf16[8,8,16,128]{3,2,1,0:T(8,128)(2,1)S(1)}, u32[]{:S(2)}, u32[]{:S(2)}) collective-permute-start(bf16[8,8,16,128]{3,2,1,0:T(8,128)(2,1)S(1)} %slice.4), channel_id=1, source_target_pairs={{0,8},{8,16},{16,24},{24,32},{32,40},{40,48},{48,56},{56,64},{64,7... | collective-permute-start | bytes 786440 | tf_op jit(solution)/shard_map/ppermute | solution.py:34
  35.4 7.9 %collective-permute-done.edge_ref = bf16[8,8,16,128]{3,2,1,0:T(8,128)(2,1)S(1)} collective-permute-done((bf16[8,8,16,128]{3,2,1,0:T(8,128)(2,1)S(1)}, bf16[8,8,16,128]{3,2,1,0:T(8,128)(2,1)S(1)}, u32[]{:S(2)}, u32[]{:S(2)}) %collective-permute-start) | collective-permute-done | bytes 262176 | tf_op jit(solution)/shard_map/ppermute | solution.py:34
  43.3 0.0 copy-done.1
  43.3 0.0 copy-start.2
  43.3 0.7 %copy-done.2 = bf16[8,8,16,128]{3,2,1,0:T(8,128)(2,1)} copy-done((bf16[8,8,16,128]{3,2,1,0:T(8,128)(2,1)}, bf16[8,8,16,128]{3,2,1,0:T(8,128)(2,1)S(1)}, u32[]{:S(2)}) %copy-start.2) | copy-done | bytes 262168
  44.0 6.2 %cross.1 = f32[8,2,2,256,128]{4,3,2,1,0:T(8,128)} custom-call(bf16[8,8,16,256]{3,2,1,0:T(8,128)(2,1)} %copy-done.1, bf16[8,8,16,128]{3,2,1,0:T(8,128)(2,1)} %copy-done.2), custom_call_target="tpu_custom_call" | custom-call | tf_op jit(solution)/shard_map/cross/pallas_call | solution.py:126
  (1 shorter events, 0.0 us)
Async XLA Ops:
  0.0 2.2 %copy-start = (bf16[1024,2000]{1,0:T(8,128)(2,1)S(1)}, bf16[1024,2000]{1,0:T(8,128)(2,1)}, u32[]{:S(2)}) copy-start(bf16[1024,2000]{1,0:T(8,128)(2,1)} %constant.2.clone.table_ref) | copy-start | bytes 12288004
  33.4 9.9 %copy-start.1 = (bf16[8,8,16,256]{3,2,1,0:T(8,128)(2,1)}, bf16[8,8,16,256]{3,2,1,0:T(8,128)(2,1)S(1)}, u32[]{:S(2)}) copy-start(bf16[8,8,16,256]{3,2,1,0:T(8,128)(2,1)S(1)} %all_to_all.5.own_ref) | copy-start | bytes 1572868
  33.5 9.8 %collective-permute-start = (bf16[8,8,16,128]{3,2,1,0:T(8,128)(2,1)S(1)}, bf16[8,8,16,128]{3,2,1,0:T(8,128)(2,1)S(1)}, u32[]{:S(2)}, u32[]{:S(2)}) collective-permute-start(bf16[8,8,16,128]{3,2,1,0:T(8,128)(2,1)S(1)} %slice.4), channel_id=1, source_target_pairs={{0,8},{8,16},{16,24},{24,32},{32,40},{40,48},{48,56},{56,64},{64,7... | collective-permute-start | bytes 786440 | tf_op jit(solution)/shard_map/ppermute | solution.py:34
  43.3 0.7 %copy-start.2 = (bf16[8,8,16,128]{3,2,1,0:T(8,128)(2,1)}, bf16[8,8,16,128]{3,2,1,0:T(8,128)(2,1)S(1)}, u32[]{:S(2)}) copy-start(bf16[8,8,16,128]{3,2,1,0:T(8,128)(2,1)S(1)} %collective-permute-done.edge_ref) | copy-start | bytes 786436

commit v2 on v0

v2 whole, which is shorter than its diff:
```python
import functools

import jax
import jax.numpy as jnp
import numpy as np
from jax import lax
from jax.experimental import pallas as pl
from jax.experimental.pallas import tpu as pltpu
from jax.sharding import PartitionSpec as P

SAMPLES = 2000
HALF = SAMPLES // 2
WIDE = 512
BINS = 64
FIRST_BIN = 40
BLOCK = 128
NEAR = 72
AHEAD = 3
OWN_BINS = 4
EDGE_BINS = 8


def make_tables():
    sample = np.arange(SAMPLES, dtype=np.int32)
    freq = np.arange(1, WIDE + 1, dtype=np.int32)
    phase = freq[:, None] * sample[None, :] % SAMPLES
    angle = np.float32(2.0 * np.pi / SAMPLES) * phase.astype(np.float32)
    real_part, imag_part = np.cos(angle), -np.sin(angle)
    high = FIRST_BIN + BINS
    near = np.r_[FIRST_BIN:high, high, FIRST_BIN - 1, high + 1 : high + NEAR - BINS - 1]
    far = np.setdiff1d(np.arange(WIDE), near)
    even, odd = far[freq[far] % 2 == 0], far[freq[far] % 2 == 1]
    pick = lambda rows, count: np.concatenate([real_part[rows, :count], imag_part[rows, :count]])
    return [
        jnp.asarray(pick(rows, count).astype(jnp.bfloat16))
        for rows, count in ((near, SAMPLES), (even, HALF), (odd, HALF))
    ]


def shifted(value, axis, steps):
    count = lax.axis_size(axis)
    return lax.ppermute(value, axis, [(source, source + steps) for source in range(count - steps)])


def product(left, right):
    return jnp.dot(left, right, preferred_element_type=jnp.float32)


def squares(value):
    return jnp.sum((value * value).reshape(-1, 8, value.shape[-1]), axis=0)


def spectra_kernel(
    near_hbm, even_hbm, odd_hbm, record_hbm, out_ref,
    near_ref, even_ref, odd_ref, record_ref, white_ref, table_sems, record_sems,
):
    recs, _, chans = record_ref.shape

    def record_copy(rec):
        return pltpu.make_async_copy(record_hbm.at[rec], record_ref.at[rec], record_sems.at[rec])

    table_copies = [
        pltpu.make_async_copy(source, target, table_sems.at[index])
        for index, (source, target) in enumerate(
            ((near_hbm, near_ref), (even_hbm, even_ref), (odd_hbm, odd_ref))
        )
    ]
    record_copy(0).start()
    for copy in table_copies:
        copy.start()
    for rec in range(1, min(AHEAD, recs)):
        record_copy(rec).start()

    def one_record(rec, ready):
        record_copy(rec).wait()
        ready(0)
        near = product(near_ref[...], record_ref[rec])
        low, high = record_ref[rec, :HALF], record_ref[rec, HALF:]
        ready(1)
        total = squares(product(even_ref[...], low + high))
        ready(2)
        total += squares(product(odd_ref[...], low - high))
        real_part, imag_part = near[:NEAR], near[NEAR:]
        power = real_part * real_part + imag_part * imag_part
        total += jnp.sum(power.reshape(-1, 8, chans), axis=0)
        level = jnp.sum(total, axis=0, keepdims=True) * (1.0 / WIDE)
        above = power[1 : BINS + 1]
        below = jnp.concatenate([power[BINS + 1 : BINS + 2], power[: BINS - 1]], axis=0)
        scale = lax.rsqrt(0.5 * ((below + power[:BINS] + above) / 3.0) + level + 1e-06)
        white = real_part[:BINS] * scale, imag_part[:BINS] * scale
        first = rec * 2 * BINS
        if not isinstance(rec, int):
            first = pl.multiple_of(first, 2 * BINS)
        for part in range(2):
            for block in range(chans // BLOCK):
                lanes = slice(block * BLOCK, (block + 1) * BLOCK)
                white_ref[block, pl.ds(first + part * BINS, BINS), :] = white[part][:, lanes]

    def later_record(rec, _):
        @pl.when(rec + AHEAD - 1 < recs)
        def _():
            record_copy(rec + AHEAD - 1).start()

        one_record(rec, lambda index: None)
        return 0

    one_record(0, lambda index: table_copies[index].wait())
    lax.fori_loop(1, recs, later_record, 0)
    for index in range(BINS):
        for block in range(chans // BLOCK):
            both = [
                white_ref[block, pl.ds(index + part * BINS, recs, stride=2 * BINS), :]
                for part in range(2)
            ]
            lanes = slice(block * BLOCK, (block + 1) * BLOCK)
            out_ref[index, :, lanes] = jnp.concatenate(both, axis=0).astype(jnp.bfloat16)


def spectra(tables, record):
    recs, samples, chans = record.shape
    rows = sum(table.shape[0] * table.shape[1] for table in tables)
    return pl.pallas_call(
        spectra_kernel,
        in_specs=[pl.BlockSpec(memory_space=pltpu.HBM)] * 4,
        out_specs=pl.BlockSpec(memory_space=pltpu.VMEM),
        out_shape=jax.ShapeDtypeStruct((BINS, 2 * recs, chans), jnp.bfloat16),
        scratch_shapes=[pltpu.VMEM(table.shape, table.dtype) for table in tables]
        + [
            pltpu.VMEM(record.shape, jnp.bfloat16),
            pltpu.VMEM((chans // BLOCK, recs * 2 * BINS, BLOCK), jnp.float32),
            pltpu.SemaphoreType.DMA((3,)),
            pltpu.SemaphoreType.DMA((recs,)),
        ],
        compiler_params=pltpu.CompilerParams(vmem_limit_bytes=60 * 2**20),
        cost_estimate=pl.CostEstimate(
            flops=2 * recs * chans * rows,
            bytes_accessed=2 * (recs * samples * chans + rows),
            transcendentals=recs * chans * BINS,
        ),
        name="spectra",
    )(*tables, record)


def turned(value):
    recs = value.shape[1] // 2
    wide = value.astype(jnp.float32)
    other = jnp.concatenate([wide[:, recs:], -wide[:, :recs]], axis=1)
    return other.astype(jnp.bfloat16)


def flat(value):
    return value.reshape(-1, value.shape[-1])


def against(left, right):
    return lax.dot_general(left, right, (((0,), (0,)), ((), ())), preferred_element_type=jnp.float32)


def own_kernel(scale, own_ref, out_ref):
    bins = out_ref.shape[0]
    for bin_at in range(bins):
        own = own_ref[:, pl.program_id(0) * bins + bin_at]
        both = flat(own), flat(turned(own))
        for block in range(own.shape[-1] // BLOCK):
            here = slice(block * BLOCK, (block + 1) * BLOCK)
            first = max(block - 1, 0) * BLOCK
            for part in range(2):
                sums = against(both[part][:, here], both[0][:, first : (block + 1) * BLOCK]) * scale
                out_ref[bin_at, 0, part, here, :] = sums[:, -BLOCK:]
                if block:
                    out_ref[bin_at, 1, part, here, :] = sums[:, :BLOCK]


def edge_kernel(scale, own_ref, edge_ref, _, out_ref):
    bins = out_ref.shape[0]
    for bin_at in range(bins):
        row = pl.program_id(0) * bins + bin_at
        own = own_ref[:, row, :, :BLOCK]
        edge = flat(edge_ref[:, row])
        both = flat(own), flat(turned(own))
        for part in range(2):
            out_ref[bin_at, 0, part] = against(both[part], edge) * scale


def own_stack(own, records):
    groups, freqs, depth, chans = own.shape
    return pl.pallas_call(
        functools.partial(own_kernel, 1.0 / records),
        grid=(freqs // OWN_BINS,),
        in_specs=[pl.BlockSpec(memory_space=pltpu.VMEM)],
        out_specs=pl.BlockSpec((OWN_BINS, 2, 2, chans, BLOCK), lambda f: (f, 0, 0, 0, 0)),
        out_shape=jax.ShapeDtypeStruct((freqs, 2, 2, chans, BLOCK), jnp.float32),
        compiler_params=pltpu.CompilerParams(vmem_limit_bytes=16 * 2**20),
        cost_estimate=pl.CostEstimate(
            flops=2 * freqs * chans * groups * depth * 3 * BLOCK,
            bytes_accessed=freqs * 4 * chans * BLOCK * 4,
            transcendentals=0,
        ),
        name="own",
    )(own)


def edge_stack(own, edge, stack, records):
    groups, freqs, depth, chans = own.shape
    return pl.pallas_call(
        functools.partial(edge_kernel, 1.0 / records),
        grid=(freqs // EDGE_BINS,),
        in_specs=[pl.BlockSpec(memory_space=pltpu.VMEM)] * 2 + [pl.BlockSpec(memory_space=pl.ANY)],
        out_specs=pl.BlockSpec((EDGE_BINS, 1, 2, BLOCK, BLOCK), lambda f: (f, 1, 0, 0, 0)),
        out_shape=jax.ShapeDtypeStruct(stack.shape, stack.dtype),
        input_output_aliases={2: 0},
        compiler_params=pltpu.CompilerParams(vmem_limit_bytes=16 * 2**20),
        cost_estimate=pl.CostEstimate(
            flops=2 * freqs * BLOCK * groups * depth * 2 * BLOCK,
            bytes_accessed=freqs * 2 * BLOCK * BLOCK * 4,
            transcendentals=0,
        ),
        name="edge",
    )(own, edge, stack)


def shards(record):
    chans, recs, _ = record.shape
    groups = lax.axis_size("rec")
    records = float(recs * groups)
    white = spectra(make_tables(), record.transpose(1, 2, 0))
    white = white.reshape(groups, BINS // groups, 2 * recs, chans)
    own = lax.all_to_all(white, "rec", 0, 0, tiled=True)
    edge = shifted(own[..., chans - BLOCK :], "chan", 1)
    return edge_stack(own, edge, own_stack(own, records), records)


def solution(mesh):
    in_specs = (P("chan", "rec", None),)
    out_specs = P("rec", None, None, "chan", None)
    return jax.shard_map(shards, mesh=mesh, in_specs=in_specs, out_specs=out_specs, check_vma=False)
```

time: 458 us -> 40.3 us (0.09)
  waiting for transfers between devices: 373 us -> 5.43 us
  other arithmetic: 32.6 us -> 0 us
  blocking collectives: 0 us -> 18.5 us
  local copies, waits for them, and re-layouts: 18.1 us -> 0.05 us
  matrix products: 17.2 us -> 0 us
  Pallas kernels: 0 us -> 14.2 us
  between operations: 13.5 us -> 0.02 us
    reduce_scatter x1 -> x0, waiting for transfers between devices: 364 us -> none  [shards(): lax.psum_scatter(cross_stack(spectra, edge, records), 'rec', scatter_dime...]
    all_to_all x0 -> x1, blocking collectives: none -> 18.5 us  [shards(): own = lax.all_to_all(white, 'rec', 0, 0, tiled=True)]
    another operation x3 -> x0, other arithmetic: 18.4 us -> none
    dot_general x5 -> x0, matrix products: 17.2 us -> none  [the longest x1 12 us: shards(): jnp.dot(record.reshape(chans * recs, samples), table, preferred_element_t...]
    pallas_call x0 -> x3, Pallas kernels: none -> 14.2 us  [the longest x1 10.4 us: spectra(): pl.pallas_call(spectra_kernel, in_specs=[pl.BlockSpec(memory_space=pltpu....]
    unnamed x1 -> x0, local copies, waits for them, and re-layouts: 12.5 us -> none
    div x2 -> x0, other arithmetic: 11.1 us -> none  [the longest x1 11.1 us: cross_stack(): return result.reshape(freqs, 2, 2, chans, width) / records]
  transfers between devices with their start and end apart: 2 -> 1, of which waited for: 2 -> 1; matrix products, arithmetic and copies ran while one was open for 0% -> 0% of each run, Pallas kernels for 0% -> 6%
where the time goes in v2:
time: 40.3 us; the launch traced here: 40.1 us
  blocking collectives  18.5 us (46%)
  Pallas kernels  14.2 us (35%)
  waiting for transfers between devices  5.43 us (13%)
  starting transfers between devices  1.92 us (5%)
    all_to_all x1, blocking collectives, shards(): own = lax.all_to_all(white, 'rec', 0, 0, tiled=True)  18.5 us
    pallas_call x1, Pallas kernels, spectra(): pl.pallas_call(spectra_kernel, in_specs=[pl.BlockSpec(memory_space=pltpu....  10.4 us
    ppermute x1, waiting for transfers between devices, shifted(): lax.ppermute(value, axis, [(source, source + steps) for source in range(c...  5.43 us
    pallas_call x1, Pallas kernels, own_stack(): pl.pallas_call(functools.partial(own_kernel, 1.0 / records), grid=(freqs...  2.44 us
    ppermute x1, starting transfers between devices, shifted(): lax.ppermute(value, axis, [(source, source + steps) for source in range(c...  1.92 us
    pallas_call x1, Pallas kernels, edge_stack(): pl.pallas_call(functools.partial(edge_kernel, 1.0 / records), grid=(freqs...  1.31 us
  transfers between devices with their start and end apart: 1, of which 1 were waited for; matrix products, arithmetic and copies ran while one was open for 0% of the time, Pallas kernels for 6%

profile of v2, /device:TPU:128, one launch (start us, length us, event | category | flops | bytes accessed | tf_op | source)
XLA Modules:
  0.0 40.1 jit_solution(10126152724993621762)
XLA Ops:
  0.0 10.4 %spectra.1 = bf16[64,16,256]{2,1,0:T(8,128)(2,1)} custom-call(bf16[144,2000]{1,0:T(8,128)(2,1)} %constant.6.clone.near_hbm, bf16[440,1000]{1,0:T(8,128)(2,1)} %constant.7.clone.even_hbm, bf16[440,1000]{1,0:T(8,128)(2,1)} %constant.8.clone.odd_hbm, bf16[8,2000,256]{2,1,0:T(8,128)(2,1)} %bitcast.3), custom_call_target="tpu_custom_call" | custom-call | flops 4784128000 | bytes 10528000 | tf_op jit(solution)/shard_map/spectra/pallas_call | solution.py:122
  10.4 18.5 %all_to_all.5.own_ref = bf16[8,8,16,256]{3,2,1,0:T(8,128)(2,1)S(1)} all-to-all(bf16[8,8,16,256]{3,2,1,0:T(8,128)(2,1)} %bitcast.2), channel_id=1, replica_groups=mesh['chan'=32,'rec'=8] {'rec'}, dimensions={0} | all-to-all | bytes 1048576 | tf_op jit(solution)/shard_map/all_to_all | solution.py:228
  29.0 1.9 %collective-permute-start = (bf16[8,8,16,128]{3,2,1,0:T(8,128)(2,1)S(1)}, bf16[8,8,16,128]{3,2,1,0:T(8,128)(2,1)S(1)}, u32[]{:S(2)}, u32[]{:S(2)}) collective-permute-start(bf16[8,8,16,128]{3,2,1,0:T(8,128)(2,1)S(1)} %slice.4), channel_id=1, source_target_pairs={{0,8},{8,16},{16,24},{24,32},{32,40},{40,48},{48,56},{56,64},{64,7... | collective-permute-start | bytes 786440 | tf_op jit(solution)/shard_map/ppermute | solution.py:42
  30.9 2.4 %own.1._ = f32[8,2,2,256,128]{4,3,2,1,0:T(8,128)} custom-call(bf16[8,8,16,256]{3,2,1,0:T(8,128)(2,1)S(1)} %all_to_all.5.own_ref), custom_call_target="tpu_custom_call" | custom-call | flops 201326592 | bytes 4194304 | tf_op jit(solution)/shard_map/own/pallas_call | solution.py:187
  33.4 5.4 %collective-permute-done.edge_ref = bf16[8,8,16,128]{3,2,1,0:T(8,128)(2,1)S(1)} collective-permute-done((bf16[8,8,16,128]{3,2,1,0:T(8,128)(2,1)S(1)}, bf16[8,8,16,128]{3,2,1,0:T(8,128)(2,1)S(1)}, u32[]{:S(2)}, u32[]{:S(2)}) %collective-permute-start) | collective-permute-done | bytes 262176 | tf_op jit(solution)/shard_map/ppermute | solution.py:42
  38.8 1.3 %edge.1 = f32[8,2,2,256,128]{4,3,2,1,0:T(8,128)} custom-call(bf16[8,8,16,256]{3,2,1,0:T(8,128)(2,1)S(1)} %all_to_all.5.own_ref, bf16[8,8,16,128]{3,2,1,0:T(8,128)(2,1)S(1)} %collective-permute-done.edge_ref, f32[8,2,2,256,128]{4,3,2,1,0:T(8,128)} %own.1._), custom_call_target="tpu_custom_call", output_to_operand_aliasing={{}: (2, {})} | custom-call | flops 67108864 | bytes 1048576 | tf_op jit(solution)/shard_map/edge/pallas_call | solution.py:205
  (1 shorter events, 0.0 us)
Async XLA Ops:
  29.0 9.8 %collective-permute-start = (bf16[8,8,16,128]{3,2,1,0:T(8,128)(2,1)S(1)}, bf16[8,8,16,128]{3,2,1,0:T(8,128)(2,1)S(1)}, u32[]{:S(2)}, u32[]{:S(2)}) collective-permute-start(bf16[8,8,16,128]{3,2,1,0:T(8,128)(2,1)S(1)} %slice.4), channel_id=1, source_target_pairs={{0,8},{8,16},{16,24},{24,32},{32,40},{40,48},{48,56},{56,64},{64,7... | collective-permute-start | bytes 786440 | tf_op jit(solution)/shard_map/ppermute | solution.py:42

commit v3 on v2

--- a/solution.py
+++ b/solution.py
@@ -10,6 +10,7 @@
 
 SAMPLES = 2000
 HALF = SAMPLES // 2
+QUARTER = SAMPLES // 4
 WIDE = 512
 BINS = 64
 FIRST_BIN = 40
@@ -29,17 +30,24 @@
     high = FIRST_BIN + BINS
     near = np.r_[FIRST_BIN:high, high, FIRST_BIN - 1, high + 1 : high + NEAR - BINS - 1]
     far = np.setdiff1d(np.arange(WIDE), near)
-    even, odd = far[freq[far] % 2 == 0], far[freq[far] % 2 == 1]
-    pick = lambda rows, count: np.concatenate([real_part[rows, :count], imag_part[rows, :count]])
-    return [
-        jnp.asarray(pick(rows, count).astype(jnp.bfloat16))
-        for rows, count in ((near, SAMPLES), (even, HALF), (odd, HALF))
-    ]
-
-
-def shifted(value, axis, steps):
+    rest = freq[far] % 4
+    parts = (
+        (near, SAMPLES),
+        (far[rest == 0], QUARTER),
+        (far[rest == 2], QUARTER),
+        (far[rest % 2 == 1], HALF),
+    )
+    tables = []
+    for bins, count in parts:
+        rows = np.concatenate([real_part[bins, :count], imag_part[bins, :count]])
+        rows = np.pad(rows, ((0, -len(rows) % 16), (0, 0)))
+        tables.append(jnp.asarray(rows.astype(jnp.bfloat16)))
+    return tables
+
+
+def turned_on(value, axis):
     count = lax.axis_size(axis)
-    return lax.ppermute(value, axis, [(source, source + steps) for source in range(count - steps)])
+    return lax.ppermute(value, axis, [(source, (source + 1) % count) for source in range(count)])
 
 
 def product(left, right):
@@ -51,19 +59,19 @@
 
 
 def spectra_kernel(
-    near_hbm, even_hbm, odd_hbm, record_hbm, out_ref,
-    near_ref, even_ref, odd_ref, record_ref, white_ref, table_sems, record_sems,
+    near_hbm, fours_hbm, twos_hbm, odds_hbm, record_hbm, out_ref,
+    near_ref, fours_ref, twos_ref, odds_ref, record_ref, white_ref, table_sems, record_sems,
 ):
     recs, _, chans = record_ref.shape
+    tables_hbm = near_hbm, fours_hbm, twos_hbm, odds_hbm
+    tables = near_ref, fours_ref, twos_ref, odds_ref
 
     def record_copy(rec):
         return pltpu.make_async_copy(record_hbm.at[rec], record_ref.at[rec], record_sems.at[rec])
 
     table_copies = [
         pltpu.make_async_copy(source, target, table_sems.at[index])
-        for index, (source, target) in enumerate(
-            ((near_hbm, near_ref), (even_hbm, even_ref), (odd_hbm, odd_ref))
-        )
+        for index, (source, target) in enumerate(zip(tables_hbm, tables))
     ]
     record_copy(0).start()
     for copy in table_copies:
@@ -76,10 +84,14 @@
         ready(0)
         near = product(near_ref[...], record_ref[rec])
         low, high = record_ref[rec, :HALF], record_ref[rec, HALF:]
+        both = low + high
+        low_both, high_both = both[:QUARTER], both[QUARTER:]
         ready(1)
-        total = squares(product(even_ref[...], low + high))
+        total = squares(product(fours_ref[...], low_both + high_both))
         ready(2)
-        total += squares(product(odd_ref[...], low - high))
+        total += squares(product(twos_ref[...], low_both - high_both))
+        ready(3)
+        total += squares(product(odds_ref[...], low - high))
         real_part, imag_part = near[:NEAR], near[NEAR:]
         power = real_part * real_part + imag_part * imag_part
         total += jnp.sum(power.reshape(-1, 8, chans), axis=0)
@@ -121,14 +133,14 @@
     rows = sum(table.shape[0] * table.shape[1] for table in tables)
     return pl.pallas_call(
         spectra_kernel,
-        in_specs=[pl.BlockSpec(memory_space=pltpu.HBM)] * 4,
+        in_specs=[pl.BlockSpec(memory_space=pltpu.HBM)] * (len(tables) + 1),
         out_specs=pl.BlockSpec(memory_space=pltpu.VMEM),
         out_shape=jax.ShapeDtypeStruct((BINS, 2 * recs, chans), jnp.bfloat16),
         scratch_shapes=[pltpu.VMEM(table.shape, table.dtype) for table in tables]
         + [
             pltpu.VMEM(record.shape, jnp.bfloat16),
             pltpu.VMEM((chans // BLOCK, recs * 2 * BINS, BLOCK), jnp.float32),
-            pltpu.SemaphoreType.DMA((3,)),
+            pltpu.SemaphoreType.DMA((len(tables),)),
             pltpu.SemaphoreType.DMA((recs,)),
         ],
         compiler_params=pltpu.CompilerParams(vmem_limit_bytes=60 * 2**20),
@@ -171,15 +183,16 @@
                     out_ref[bin_at, 1, part, here, :] = sums[:, :BLOCK]
 
 
-def edge_kernel(scale, own_ref, edge_ref, _, out_ref):
+def edge_kernel(scale, place_ref, own_ref, edge_ref, _, out_ref):
     bins = out_ref.shape[0]
+    inside = place_ref[0] > 0
     for bin_at in range(bins):
         row = pl.program_id(0) * bins + bin_at
         own = own_ref[:, row, :, :BLOCK]
         edge = flat(edge_ref[:, row])
         both = flat(own), flat(turned(own))
         for part in range(2):
-            out_ref[bin_at, 0, part] = against(both[part], edge) * scale
+            out_ref[bin_at, 0, part] = jnp.where(inside, against(both[part], edge) * scale, 0.0)
 
 
 def own_stack(own, records):
@@ -200,15 +213,20 @@
     )(own)
 
 
-def edge_stack(own, edge, stack, records):
+def edge_stack(place, own, edge, stack, records):
     groups, freqs, depth, chans = own.shape
     return pl.pallas_call(
         functools.partial(edge_kernel, 1.0 / records),
         grid=(freqs // EDGE_BINS,),
-        in_specs=[pl.BlockSpec(memory_space=pltpu.VMEM)] * 2 + [pl.BlockSpec(memory_space=pl.ANY)],
+        in_specs=[
+            pl.BlockSpec(memory_space=pltpu.SMEM),
+            pl.BlockSpec(memory_space=pltpu.VMEM),
+            pl.BlockSpec(memory_space=pltpu.VMEM),
+            pl.BlockSpec(memory_space=pl.ANY),
+        ],
         out_specs=pl.BlockSpec((EDGE_BINS, 1, 2, BLOCK, BLOCK), lambda f: (f, 1, 0, 0, 0)),
         out_shape=jax.ShapeDtypeStruct(stack.shape, stack.dtype),
-        input_output_aliases={2: 0},
+        input_output_aliases={3: 0},
         compiler_params=pltpu.CompilerParams(vmem_limit_bytes=16 * 2**20),
         cost_estimate=pl.CostEstimate(
             flops=2 * freqs * BLOCK * groups * depth * 2 * BLOCK,
@@ -216,7 +234,7 @@
             transcendentals=0,
         ),
         name="edge",
-    )(own, edge, stack)
+    )(place, own, edge, stack)
 
 
 def shards(record):
@@ -226,8 +244,9 @@
     white = spectra(make_tables(), record.transpose(1, 2, 0))
     white = white.reshape(groups, BINS // groups, 2 * recs, chans)
     own = lax.all_to_all(white, "rec", 0, 0, tiled=True)
-    edge = shifted(own[..., chans - BLOCK :], "chan", 1)
-    return edge_stack(own, edge, own_stack(own, records), records)
+    edge = turned_on(own[..., chans - BLOCK :], "chan")
+    place = lax.axis_index("chan").reshape(1)
+    return edge_stack(place, own, edge, own_stack(own, records), records)
 
 
 def solution(mesh):

time: 40.3 us -> 37.6 us (0.933)
  starting transfers between devices: 1.92 us -> 0.08 us
  Pallas kernels: 14.2 us -> 13.3 us
    ppermute x1, starting transfers between devices: 1.92 us -> 0.08 us  [turned_on(): lax.ppermute(value, axis, [(source, (source + 1) % count) for source in r...]
    pallas_call x1, Pallas kernels: 10.4 us -> 9.56 us  [spectra(): pl.pallas_call(spectra_kernel, in_specs=[pl.BlockSpec(memory_space=pltpu....]
  transfers between devices with their start and end apart: 1 -> 1, of which waited for: 1 -> 1; matrix products, arithmetic and copies ran while one was open for 0% -> 0% of each run, Pallas kernels for 6% -> 7%
where the time goes in v3:
time: 37.6 us; the launch traced here: 37.4 us
  blocking collectives  18.5 us (49%)
  Pallas kernels  13.3 us (35%)
  waiting for transfers between devices  5.44 us (14%)
    all_to_all x1, blocking collectives, shards(): own = lax.all_to_all(white, 'rec', 0, 0, tiled=True)  18.5 us
    pallas_call x1, Pallas kernels, spectra(): pl.pallas_call(spectra_kernel, in_specs=[pl.BlockSpec(memory_space=pltpu....  9.56 us
    ppermute x1, waiting for transfers between devices, turned_on(): lax.ppermute(value, axis, [(source, (source + 1) % count) for source in r...  5.44 us
    pallas_call x1, Pallas kernels, own_stack(): pl.pallas_call(functools.partial(own_kernel, 1.0 / records), grid=(freqs...  2.44 us
    pallas_call x1, Pallas kernels, edge_stack(): pl.pallas_call(functools.partial(edge_kernel, 1.0 / records), grid=(freqs...  1.32 us
  transfers between devices with their start and end apart: 1, of which 1 were waited for; matrix products, arithmetic and copies ran while one was open for 0% of the time, Pallas kernels for 7%

profile of v3, /device:TPU:128, one launch (start us, length us, event | category | flops | bytes accessed | tf_op | source)
XLA Modules:
  0.0 37.4 jit_solution(5875653035511513819)
XLA Ops:
  0.0 9.6 %spectra.1 = bf16[64,16,256]{2,1,0:T(8,128)(2,1)} custom-call(bf16[144,2000]{1,0:T(8,128)(2,1)} %constant.14.clone.near_hbm, bf16[224,500]{1,0:T(8,128)(2,1)} %constant.15.clone.fours_hbm, bf16[224,500]{1,0:T(8,128)(2,1)} %constant.16.clone.twos_hbm, bf16[448,1000]{1,0:T(8,128)(2,1)} %constant.17.clone.odds_hbm, bf16[8,2000,256]{2,1,0:T(8,128)(2,1)} %bitcast.4), custom_call_target="tpu_custom_call" | custom-call | flops 3932160000 | bytes 10112000 | tf_op jit(solution)/shard_map/spectra/pallas_call | solution.py:134
  9.6 18.5 %all_to_all.5.own_ref = bf16[8,8,16,256]{3,2,1,0:T(8,128)(2,1)S(1)} all-to-all(bf16[8,8,16,256]{3,2,1,0:T(8,128)(2,1)} %bitcast.3), channel_id=1, replica_groups=mesh['chan'=32,'rec'=8] {'rec'}, dimensions={0} | all-to-all | bytes 1048576 | tf_op jit(solution)/shard_map/all_to_all | solution.py:246
  28.1 0.1 collective-permute-start
  28.2 2.4 %own.1._ = f32[8,2,2,256,128]{4,3,2,1,0:T(8,128)} custom-call(bf16[8,8,16,256]{3,2,1,0:T(8,128)(2,1)S(1)} %all_to_all.5.own_ref), custom_call_target="tpu_custom_call" | custom-call | flops 201326592 | bytes 4194304 | tf_op jit(solution)/shard_map/own/pallas_call | solution.py:200
  30.7 5.4 %collective-permute-done.edge_ref = bf16[8,8,16,128]{3,2,1,0:T(8,128)(2,1)S(1)} collective-permute-done((bf16[8,8,16,128]{3,2,1,0:T(8,128)(2,1)S(1)}, bf16[8,8,16,128]{3,2,1,0:T(8,128)(2,1)S(1)}, u32[]{:S(2)}, u32[]{:S(2)}) %collective-permute-start) | collective-permute-done | bytes 262176 | tf_op jit(solution)/shard_map/ppermute | solution.py:50
  36.1 1.3 %edge.1 = f32[8,2,2,256,128]{4,3,2,1,0:T(8,128)} custom-call(s32[1]{0:T(128)} %bitcast.place_ref, bf16[8,8,16,256]{3,2,1,0:T(8,128)(2,1)S(1)} %all_to_all.5.own_ref, bf16[8,8,16,128]{3,2,1,0:T(8,128)(2,1)S(1)} %collective-permute-done.edge_ref, f32[8,2,2,256,128]{4,3,2,1,0:T(8,128)} %own.1._), custom_call_target="tpu_custom_call", output_to_operand_aliasing={{}: (3, {})} | custom-call | flops 67108864 | bytes 1048576 | tf_op jit(solution)/shard_map/edge/pallas_call | solution.py:218
  (1 shorter events, 0.0 us)
Async XLA Ops:
  28.1 8.0 %collective-permute-start = (bf16[8,8,16,128]{3,2,1,0:T(8,128)(2,1)S(1)}, bf16[8,8,16,128]{3,2,1,0:T(8,128)(2,1)S(1)}, u32[]{:S(2)}, u32[]{:S(2)}) collective-permute-start(bf16[8,8,16,128]{3,2,1,0:T(8,128)(2,1)S(1)} %slice.4), channel_id=1, source_target_pairs={{0,8},{8,16},{16,24},{24,32},{32,40},{40,48},{48,56},{56,64},{64,7... | collective-permute-start | bytes 786440 | tf_op jit(solution)/shard_map/ppermute | solution.py:50

commit v4 on v3

--- a/solution.py
+++ b/solution.py
@@ -60,7 +60,8 @@
 
 def spectra_kernel(
     near_hbm, fours_hbm, twos_hbm, odds_hbm, record_hbm, out_ref,
-    near_ref, fours_ref, twos_ref, odds_ref, record_ref, white_ref, table_sems, record_sems,
+    near_ref, fours_ref, twos_ref, odds_ref, record_ref, found_ref, total_ref, white_ref, table_sems,
+    record_sems,
 ):
     recs, _, chans = record_ref.shape
     tables_hbm = near_hbm, fours_hbm, twos_hbm, odds_hbm
@@ -76,22 +77,11 @@
     record_copy(0).start()
     for copy in table_copies:
         copy.start()
-    for rec in range(1, min(AHEAD, recs)):
-        record_copy(rec).start()
-
-    def one_record(rec, ready):
-        record_copy(rec).wait()
-        ready(0)
-        near = product(near_ref[...], record_ref[rec])
-        low, high = record_ref[rec, :HALF], record_ref[rec, HALF:]
-        both = low + high
-        low_both, high_both = both[:QUARTER], both[QUARTER:]
-        ready(1)
-        total = squares(product(fours_ref[...], low_both + high_both))
-        ready(2)
-        total += squares(product(twos_ref[...], low_both - high_both))
-        ready(3)
-        total += squares(product(odds_ref[...], low - high))
+    record_copy(1).start()
+
+    def whiten(rec):
+        near = found_ref[rec % 2]
+        total = total_ref[rec % 2]
         real_part, imag_part = near[:NEAR], near[NEAR:]
         power = real_part * real_part + imag_part * imag_part
         total += jnp.sum(power.reshape(-1, 8, chans), axis=0)
@@ -108,16 +98,30 @@
                 lanes = slice(block * BLOCK, (block + 1) * BLOCK)
                 white_ref[block, pl.ds(first + part * BINS, BINS), :] = white[part][:, lanes]
 
-    def later_record(rec, _):
-        @pl.when(rec + AHEAD - 1 < recs)
+    def one_record(rec, _):
+        @pl.when((rec > 0) & (rec + AHEAD - 1 < recs))
         def _():
             record_copy(rec + AHEAD - 1).start()
 
-        one_record(rec, lambda index: None)
+        record_copy(rec).wait()
+        whiten(jnp.maximum(rec - 1, 0))
+        found = product(near_ref[...], record_ref[rec])
+        low, high = record_ref[rec, :HALF], record_ref[rec, HALF:]
+        both = low + high
+        low_both, high_both = both[:QUARTER], both[QUARTER:]
+        total = squares(product(fours_ref[...], low_both + high_both))
+        total += squares(product(twos_ref[...], low_both - high_both))
+        total += squares(product(odds_ref[...], low - high))
+        found_ref[rec % 2] = found
+        total_ref[rec % 2] = total
         return 0
 
-    one_record(0, lambda index: table_copies[index].wait())
-    lax.fori_loop(1, recs, later_record, 0)
+    for copy in table_copies:
+        copy.wait()
+    for rec in range(2, min(AHEAD, recs)):
+        record_copy(rec).start()
+    lax.fori_loop(0, recs, one_record, 0)
+    whiten(recs - 1)
     for index in range(BINS):
         for block in range(chans // BLOCK):
             both = [
@@ -139,6 +143,8 @@
         scratch_shapes=[pltpu.VMEM(table.shape, table.dtype) for table in tables]
         + [
             pltpu.VMEM(record.shape, jnp.bfloat16),
+            pltpu.VMEM((2, 2 * NEAR, chans), jnp.float32),
+            pltpu.VMEM((2, 8, chans), jnp.float32),
             pltpu.VMEM((chans // BLOCK, recs * 2 * BINS, BLOCK), jnp.float32),
             pltpu.SemaphoreType.DMA((len(tables),)),
             pltpu.SemaphoreType.DMA((recs,)),

time: 37.6 us -> 37.1 us (0.987)
  Pallas kernels: 13.3 us -> 12.8 us
    pallas_call x1, Pallas kernels: 9.56 us -> 9.04 us  [spectra(): pl.pallas_call(spectra_kernel, in_specs=[pl.BlockSpec(memory_space=pltpu....]
where the time goes in v4:
time: 37.1 us; the launch traced here: 36.9 us
  blocking collectives  18.5 us (50%)
  Pallas kernels  12.8 us (35%)
  waiting for transfers between devices  5.44 us (15%)
    all_to_all x1, blocking collectives, shards(): own = lax.all_to_all(white, 'rec', 0, 0, tiled=True)  18.5 us
    pallas_call x1, Pallas kernels, spectra(): pl.pallas_call(spectra_kernel, in_specs=[pl.BlockSpec(memory_space=pltpu....  9.04 us
    ppermute x1, waiting for transfers between devices, turned_on(): lax.ppermute(value, axis, [(source, (source + 1) % count) for source in r...  5.44 us
    pallas_call x1, Pallas kernels, own_stack(): pl.pallas_call(functools.partial(own_kernel, 1.0 / records), grid=(freqs...  2.44 us
    pallas_call x1, Pallas kernels, edge_stack(): pl.pallas_call(functools.partial(edge_kernel, 1.0 / records), grid=(freqs...  1.31 us
  transfers between devices with their start and end apart: 1, of which 1 were waited for; matrix products, arithmetic and copies ran while one was open for 0% of the time, Pallas kernels for 7%

profile of v4, /device:TPU:128, one launch (start us, length us, event | category | flops | bytes accessed | tf_op | source)
XLA Modules:
  0.0 36.9 jit_solution(1719986007053572806)
XLA Ops:
  0.0 9.0 %spectra.1 = bf16[64,16,256]{2,1,0:T(8,128)(2,1)} custom-call(bf16[144,2000]{1,0:T(8,128)(2,1)} %constant.14.clone.near_hbm, bf16[224,500]{1,0:T(8,128)(2,1)} %constant.15.clone.fours_hbm, bf16[224,500]{1,0:T(8,128)(2,1)} %constant.16.clone.twos_hbm, bf16[448,1000]{1,0:T(8,128)(2,1)} %constant.17.clone.odds_hbm, bf16[8,2000,256]{2,1,0:T(8,128)(2,1)} %bitcast.4), custom_call_target="tpu_custom_call" | custom-call | flops 3932160000 | bytes 10112000 | tf_op jit(solution)/shard_map/spectra/pallas_call | solution.py:138
  9.0 18.5 %all_to_all.5.own_ref = bf16[8,8,16,256]{3,2,1,0:T(8,128)(2,1)S(1)} all-to-all(bf16[8,8,16,256]{3,2,1,0:T(8,128)(2,1)} %bitcast.3), channel_id=1, replica_groups=mesh['chan'=32,'rec'=8] {'rec'}, dimensions={0} | all-to-all | bytes 1048576 | tf_op jit(solution)/shard_map/all_to_all | solution.py:252
  27.6 0.1 collective-permute-start
  27.7 2.4 %own.1._ = f32[8,2,2,256,128]{4,3,2,1,0:T(8,128)} custom-call(bf16[8,8,16,256]{3,2,1,0:T(8,128)(2,1)S(1)} %all_to_all.5.own_ref), custom_call_target="tpu_custom_call" | custom-call | flops 201326592 | bytes 4194304 | tf_op jit(solution)/shard_map/own/pallas_call | solution.py:206
  30.2 5.4 %collective-permute-done.edge_ref = bf16[8,8,16,128]{3,2,1,0:T(8,128)(2,1)S(1)} collective-permute-done((bf16[8,8,16,128]{3,2,1,0:T(8,128)(2,1)S(1)}, bf16[8,8,16,128]{3,2,1,0:T(8,128)(2,1)S(1)}, u32[]{:S(2)}, u32[]{:S(2)}) %collective-permute-start) | collective-permute-done | bytes 262176 | tf_op jit(solution)/shard_map/ppermute | solution.py:50
  35.6 1.3 %edge.1 = f32[8,2,2,256,128]{4,3,2,1,0:T(8,128)} custom-call(s32[1]{0:T(128)} %bitcast.place_ref, bf16[8,8,16,256]{3,2,1,0:T(8,128)(2,1)S(1)} %all_to_all.5.own_ref, bf16[8,8,16,128]{3,2,1,0:T(8,128)(2,1)S(1)} %collective-permute-done.edge_ref, f32[8,2,2,256,128]{4,3,2,1,0:T(8,128)} %own.1._), custom_call_target="tpu_custom_call", output_to_operand_aliasing={{}: (3, {})} | custom-call | flops 67108864 | bytes 1048576 | tf_op jit(solution)/shard_map/edge/pallas_call | solution.py:224
  (1 shorter events, 0.0 us)
Async XLA Ops:
  27.6 8.0 %collective-permute-start = (bf16[8,8,16,128]{3,2,1,0:T(8,128)(2,1)S(1)}, bf16[8,8,16,128]{3,2,1,0:T(8,128)(2,1)S(1)}, u32[]{:S(2)}, u32[]{:S(2)}) collective-permute-start(bf16[8,8,16,128]{3,2,1,0:T(8,128)(2,1)S(1)} %slice.4), channel_id=1, source_target_pairs={{0,8},{8,16},{16,24},{24,32},{32,40},{40,48},{48,56},{56,64},{64,7... | collective-permute-start | bytes 786440 | tf_op jit(solution)/shard_map/ppermute | solution.py:50

commit v5 on v4

--- a/solution.py
+++ b/solution.py
@@ -18,7 +18,7 @@
 NEAR = 72
 AHEAD = 3
 OWN_BINS = 4
-EDGE_BINS = 8
+EDGE_BINS = 4
 
 
 def make_tables():
@@ -145,7 +145,7 @@
             pltpu.VMEM(record.shape, jnp.bfloat16),
             pltpu.VMEM((2, 2 * NEAR, chans), jnp.float32),
             pltpu.VMEM((2, 8, chans), jnp.float32),
-            pltpu.VMEM((chans // BLOCK, recs * 2 * BINS, BLOCK), jnp.float32),
+            pltpu.VMEM((chans // BLOCK, (recs + 1) * 2 * BINS, BLOCK), jnp.float32),
             pltpu.SemaphoreType.DMA((len(tables),)),
             pltpu.SemaphoreType.DMA((recs,)),
         ],
@@ -174,41 +174,59 @@
     return lax.dot_general(left, right, (((0,), (0,)), ((), ())), preferred_element_type=jnp.float32)
 
 
-def own_kernel(scale, own_ref, out_ref):
+def own_kernel(scale, place_ref, own_ref, out_ref, left_ref):
     bins = out_ref.shape[0]
+    inside = place_ref[0] > 0
     for bin_at in range(bins):
         own = own_ref[:, pl.program_id(0) * bins + bin_at]
+        row = pl.program_id(0) * bins + bin_at
         both = flat(own), flat(turned(own))
         for block in range(own.shape[-1] // BLOCK):
             here = slice(block * BLOCK, (block + 1) * BLOCK)
             first = max(block - 1, 0) * BLOCK
             for part in range(2):
-                sums = against(both[part][:, here], both[0][:, first : (block + 1) * BLOCK]) * scale
+                left = both[part][:, here].T
+                if block == 0:
+                    left_ref[row, part] = jnp.where(inside, left, jnp.zeros_like(left))
+                sums = product(left, both[0][:, first : (block + 1) * BLOCK]) * scale
                 out_ref[bin_at, 0, part, here, :] = sums[:, -BLOCK:]
                 if block:
                     out_ref[bin_at, 1, part, here, :] = sums[:, :BLOCK]
 
 
-def edge_kernel(scale, place_ref, own_ref, edge_ref, _, out_ref):
-    bins = out_ref.shape[0]
-    inside = place_ref[0] > 0
+def edge_kernel(scale, first_bin, left_ref, edge_ref, _, out_ref, sums_ref, sems):
+    bins = edge_ref.shape[1]
+    copies = []
     for bin_at in range(bins):
-        row = pl.program_id(0) * bins + bin_at
-        own = own_ref[:, row, :, :BLOCK]
-        edge = flat(edge_ref[:, row])
-        both = flat(own), flat(turned(own))
+        edge = flat(edge_ref[:, bin_at])
         for part in range(2):
-            out_ref[bin_at, 0, part] = jnp.where(inside, against(both[part], edge) * scale, 0.0)
-
-
-def own_stack(own, records):
+            sums_ref[bin_at, part] = product(left_ref[first_bin + bin_at, part], edge) * scale
+        copies.append(
+            pltpu.make_async_copy(
+                sums_ref.at[bin_at],
+                out_ref.at[first_bin + bin_at, 1, :, pl.ds(0, BLOCK), :],
+                sems.at[bin_at],
+            )
+        )
+        copies[-1].start()
+    for copy in copies:
+        copy.wait()
+
+
+def own_stack(place, own, records):
     groups, freqs, depth, chans = own.shape
     return pl.pallas_call(
         functools.partial(own_kernel, 1.0 / records),
         grid=(freqs // OWN_BINS,),
-        in_specs=[pl.BlockSpec(memory_space=pltpu.VMEM)],
-        out_specs=pl.BlockSpec((OWN_BINS, 2, 2, chans, BLOCK), lambda f: (f, 0, 0, 0, 0)),
-        out_shape=jax.ShapeDtypeStruct((freqs, 2, 2, chans, BLOCK), jnp.float32),
+        in_specs=[pl.BlockSpec(memory_space=pltpu.SMEM), pl.BlockSpec(memory_space=pltpu.VMEM)],
+        out_specs=[
+            pl.BlockSpec((OWN_BINS, 2, 2, chans, BLOCK), lambda f: (f, 0, 0, 0, 0)),
+            pl.BlockSpec(memory_space=pltpu.VMEM),
+        ],
+        out_shape=[
+            jax.ShapeDtypeStruct((freqs, 2, 2, chans, BLOCK), jnp.float32),
+            jax.ShapeDtypeStruct((freqs, 2, BLOCK, groups * depth), jnp.bfloat16),
+        ],
         compiler_params=pltpu.CompilerParams(vmem_limit_bytes=16 * 2**20),
         cost_estimate=pl.CostEstimate(
             flops=2 * freqs * chans * groups * depth * 3 * BLOCK,
@@ -216,31 +234,33 @@
             transcendentals=0,
         ),
         name="own",
-    )(own)
-
-
-def edge_stack(place, own, edge, stack, records):
-    groups, freqs, depth, chans = own.shape
+    )(place, own)
+
+
+def edge_stack(first_bin, left, edge, stack, records):
+    groups, bins, depth, _ = edge.shape
     return pl.pallas_call(
-        functools.partial(edge_kernel, 1.0 / records),
-        grid=(freqs // EDGE_BINS,),
+        functools.partial(edge_kernel, 1.0 / records, first_bin),
         in_specs=[
-            pl.BlockSpec(memory_space=pltpu.SMEM),
             pl.BlockSpec(memory_space=pltpu.VMEM),
             pl.BlockSpec(memory_space=pltpu.VMEM),
             pl.BlockSpec(memory_space=pl.ANY),
         ],
-        out_specs=pl.BlockSpec((EDGE_BINS, 1, 2, BLOCK, BLOCK), lambda f: (f, 1, 0, 0, 0)),
+        out_specs=pl.BlockSpec(memory_space=pl.ANY),
         out_shape=jax.ShapeDtypeStruct(stack.shape, stack.dtype),
-        input_output_aliases={3: 0},
+        scratch_shapes=[
+            pltpu.VMEM((bins, 2, BLOCK, BLOCK), jnp.float32),
+            pltpu.SemaphoreType.DMA((bins,)),
+        ],
+        input_output_aliases={2: 0},
         compiler_params=pltpu.CompilerParams(vmem_limit_bytes=16 * 2**20),
         cost_estimate=pl.CostEstimate(
-            flops=2 * freqs * BLOCK * groups * depth * 2 * BLOCK,
-            bytes_accessed=freqs * 2 * BLOCK * BLOCK * 4,
+            flops=2 * bins * BLOCK * groups * depth * 2 * BLOCK,
+            bytes_accessed=bins * 2 * BLOCK * BLOCK * 4,
             transcendentals=0,
         ),
         name="edge",
-    )(place, own, edge, stack)
+    )(left, edge, stack)
 
 
 def shards(record):
@@ -250,9 +270,14 @@
     white = spectra(make_tables(), record.transpose(1, 2, 0))
     white = white.reshape(groups, BINS // groups, 2 * recs, chans)
     own = lax.all_to_all(white, "rec", 0, 0, tiled=True)
-    edge = turned_on(own[..., chans - BLOCK :], "chan")
+    freqs = own.shape[1]
+    firsts = range(0, freqs, EDGE_BINS)
+    edges = [turned_on(own[:, first : first + EDGE_BINS, :, chans - BLOCK :], "chan") for first in firsts]
     place = lax.axis_index("chan").reshape(1)
-    return edge_stack(place, own, edge, own_stack(own, records), records)
+    stack, left = own_stack(place, own, records)
+    for first, edge in zip(firsts, edges):
+        stack = edge_stack(first, left, edge, stack, records)
+    return stack
 
 
 def solution(mesh):

time: 37.1 us -> 36.7 us (0.989)
  waiting for transfers between devices: 5.44 us -> 3.71 us
  starting transfers between devices: 0.08 us -> 0.86 us
  Pallas kernels: 12.8 us -> 13.4 us
    ppermute x1 -> x2, waiting for transfers between devices: 5.44 us -> 3.71 us  [turned_on(): lax.ppermute(value, axis, [(source, (source + 1) % count) for source in r...]
    ppermute x1 -> x2, starting transfers between devices: 0.08 us -> 0.86 us  [turned_on(): lax.ppermute(value, axis, [(source, (source + 1) % count) for source in r...]
    pallas_call x1 -> x2, Pallas kernels: 1.31 us -> 1.95 us  [edge_stack(): pl.pallas_call(functools.partial(edge_kernel, 1.0 / records, first_bin),...]
  transfers between devices with their start and end apart: 1 -> 2, of which waited for: 1 -> 2; matrix products, arithmetic and copies ran while one was open for 0% -> 0% of each run, Pallas kernels for 7% -> 9%
where the time goes in v5:
time: 36.7 us; the launch traced here: 36.6 us
  blocking collectives  18.5 us (50%)
  Pallas kernels  13.4 us (37%)
  waiting for transfers between devices  3.71 us (10%)
  starting transfers between devices  0.86 us (2%)
    all_to_all x1, blocking collectives, shards(): own = lax.all_to_all(white, 'rec', 0, 0, tiled=True)  18.5 us
    pallas_call x1, Pallas kernels, spectra(): pl.pallas_call(spectra_kernel, in_specs=[pl.BlockSpec(memory_space=pltpu....  9.04 us
    ppermute x2, waiting for transfers between devices, turned_on(): lax.ppermute(value, axis, [(source, (source + 1) % count) for source in r...  3.71 us
    pallas_call x1, Pallas kernels, own_stack(): pl.pallas_call(functools.partial(own_kernel, 1.0 / records), grid=(freqs...  2.42 us
    pallas_call x2, Pallas kernels, edge_stack(): pl.pallas_call(functools.partial(edge_kernel, 1.0 / records, first_bin),...  1.95 us
    ppermute x2, starting transfers between devices, turned_on(): lax.ppermute(value, axis, [(source, (source + 1) % count) for source in r...  0.86 us
  transfers between devices with their start and end apart: 2, of which 2 were waited for; matrix products, arithmetic and copies ran while one was open for 0% of the time, Pallas kernels for 9%

profile of v5, /device:TPU:128, one launch (start us, length us, event | category | flops | bytes accessed | tf_op | source)
XLA Modules:
  0.0 36.6 jit_solution(17162827881980907975)
XLA Ops:
  0.0 9.0 %spectra.1 = bf16[64,16,256]{2,1,0:T(8,128)(2,1)} custom-call(bf16[144,2000]{1,0:T(8,128)(2,1)} %constant.14.clone.near_hbm, bf16[224,500]{1,0:T(8,128)(2,1)} %constant.15.clone.fours_hbm, bf16[224,500]{1,0:T(8,128)(2,1)} %constant.16.clone.twos_hbm, bf16[448,1000]{1,0:T(8,128)(2,1)} %constant.17.clone.odds_hbm, bf16[8,2000,256]{2,1,0:T(8,128)(2,1)} %bitcast.4), custom_call_target="tpu_custom_call" | custom-call | flops 3932160000 | bytes 10112000 | tf_op jit(solution)/shard_map/spectra/pallas_call | solution.py:138
  9.0 18.5 %all_to_all.5.own_ref = bf16[8,8,16,256]{3,2,1,0:T(8,128)(2,1)S(1)} all-to-all(bf16[8,8,16,256]{3,2,1,0:T(8,128)(2,1)} %bitcast.3), channel_id=1, replica_groups=mesh['chan'=32,'rec'=8] {'rec'}, dimensions={0} | all-to-all | bytes 1048576 | tf_op jit(solution)/shard_map/all_to_all | solution.py:272
  27.6 0.1 collective-permute-start.1
  27.7 0.8 %collective-permute-start = (bf16[8,4,16,128]{3,2,1,0:T(8,128)(2,1)S(1)}, bf16[8,4,16,128]{3,2,1,0:T(8,128)(2,1)S(1)}, u32[]{:S(2)}, u32[]{:S(2)}) collective-permute-start(bf16[8,4,16,128]{3,2,1,0:T(8,128)(2,1)S(1)} %get-tuple-element.10), channel_id=1, source_target_pairs={{0,8},{8,16},{16,24},{24,32},{32,40},{40,48},{48,56},{56,64},{64,7... | collective-permute-start | bytes 393224 | tf_op jit(solution)/shard_map/ppermute | solution.py:50
  28.5 2.4 %own.1 = (f32[8,2,2,256,128]{4,3,2,1,0:T(8,128)}, bf16[8,2,128,128]{3,2,1,0:T(8,128)(2,1)S(1)}) custom-call(s32[1]{0:T(128)} %bitcast.place_ref, bf16[8,8,16,256]{3,2,1,0:T(8,128)(2,1)S(1)} %all_to_all.5.own_ref), custom_call_target="tpu_custom_call" | custom-call | flops 201326592 | bytes 4194304 | tf_op jit(solution)/shard_map/own/pallas_call | solution.py:218
  30.9 3.3 %collective-permute-done.1.edge_ref = bf16[8,4,16,128]{3,2,1,0:T(8,128)(2,1)S(1)} collective-permute-done((bf16[8,4,16,128]{3,2,1,0:T(8,128)(2,1)S(1)}, bf16[8,4,16,128]{3,2,1,0:T(8,128)(2,1)S(1)}, u32[]{:S(2)}, u32[]{:S(2)}) %collective-permute-start.1) | collective-permute-done | bytes 131104 | tf_op jit(solution)/shard_map/ppermute | solution.py:50
  34.2 1.0 %edge.2._ = f32[8,2,2,256,128]{4,3,2,1,0:T(8,128)} custom-call(bf16[8,2,128,128]{3,2,1,0:T(8,128)(2,1)S(1)} %get-tuple-element.7.left_ref, bf16[8,4,16,128]{3,2,1,0:T(8,128)(2,1)S(1)} %collective-permute-done.1.edge_ref, f32[8,2,2,256,128]{4,3,2,1,0:T(8,128)} %get-tuple-element.8._), custom_call_target="tpu_custom_call", output_to_operand_aliasing={{}: (2, {})} | custom-call | flops 33554432 | bytes 524288 | tf_op jit(solution)/shard_map/edge/pallas_call | solution.py:242
  35.2 0.4 %collective-permute-done.edge_ref = bf16[8,4,16,128]{3,2,1,0:T(8,128)(2,1)S(1)} collective-permute-done((bf16[8,4,16,128]{3,2,1,0:T(8,128)(2,1)S(1)}, bf16[8,4,16,128]{3,2,1,0:T(8,128)(2,1)S(1)}, u32[]{:S(2)}, u32[]{:S(2)}) %collective-permute-start) | collective-permute-done | bytes 131104 | tf_op jit(solution)/shard_map/ppermute | solution.py:50
  35.6 1.0 %edge.3 = f32[8,2,2,256,128]{4,3,2,1,0:T(8,128)} custom-call(bf16[8,2,128,128]{3,2,1,0:T(8,128)(2,1)S(1)} %get-tuple-element.7.left_ref, bf16[8,4,16,128]{3,2,1,0:T(8,128)(2,1)S(1)} %collective-permute-done.edge_ref, f32[8,2,2,256,128]{4,3,2,1,0:T(8,128)} %edge.2._), custom_call_target="tpu_custom_call", output_to_operand_aliasing={{}: (2, {})} | custom-call | flops 33554432 | bytes 524288 | tf_op jit(solution)/shard_map/edge/pallas_call | solution.py:242
  (1 shorter events, 0.0 us)
Async XLA Ops:
  27.6 6.6 %collective-permute-start.1 = (bf16[8,4,16,128]{3,2,1,0:T(8,128)(2,1)S(1)}, bf16[8,4,16,128]{3,2,1,0:T(8,128)(2,1)S(1)}, u32[]{:S(2)}, u32[]{:S(2)}) collective-permute-start(bf16[8,4,16,128]{3,2,1,0:T(8,128)(2,1)S(1)} %get-tuple-element.9), channel_id=1, source_target_pairs={{0,8},{8,16},{16,24},{24,32},{32,40},{40,48},{48,56},{56,64},{64,7... | collective-permute-start | bytes 393224 | tf_op jit(solution)/shard_map/ppermute | solution.py:50
  27.7 7.9 %collective-permute-start = (bf16[8,4,16,128]{3,2,1,0:T(8,128)(2,1)S(1)}, bf16[8,4,16,128]{3,2,1,0:T(8,128)(2,1)S(1)}, u32[]{:S(2)}, u32[]{:S(2)}) collective-permute-start(bf16[8,4,16,128]{3,2,1,0:T(8,128)(2,1)S(1)} %get-tuple-element.10), channel_id=1, source_target_pairs={{0,8},{8,16},{16,24},{24,32},{32,40},{40,48},{48,56},{56,64},{64,7... | collective-permute-start | bytes 393224 | tf_op jit(solution)/shard_map/ppermute | solution.py:50
